TPU v7x, 512 devices: a whole 4x4x16 slice. The times are simulated.
512 devices in a mesh: seg: 64 (over x, z), grp: 4 (over y), pair: 2 (over core).
Axes of the slice: x: 4, y: 4, z: 16, core: 2. Of those that a mesh axis runs over, the one named last changes fastest.
Arguments:
- observations: float32 [2048, 256], P(('grp', 'seg')), may hold values from -6 to 6
- masks: int32 [2048, 256], P(('grp', 'seg')), may hold values 0 or 1
- gains: float32 [256], replicated, may hold values from 0.05 to 0.5
- transition: float32 [256, 256], replicated, may hold values from -1 to 1, as said below
- smoother_scale: float32 [256], replicated, may hold values from 0.995 to 0.9999
- initial_mean: float32 [256], replicated, may hold values from -8 to 8
Outputs:
- filtered: float32 [2048, 256], P(('grp', 'seg'), 'pair')
- smoothed: float32 [2048, 256], P(('grp', 'seg'), 'pair')
Inputs may be any that keep to these rules, and one draw needn't show every extreme that they name: Each column of transition is a unit vector scaled by a factor in (0, 1); the columns are orthogonal.
All inputs are finite; a program needn't handle non-finite values. No bound on the sum of `masks` on one device may be relied on, other than what follows from the above.
Results may differ from a plain program's by a relative error of at most 0.0003.
Values sent between devices are 32-bit elements; how exact they have to be, the bound alone decides.
A program may use at most 64 MiB of HBM per device.

v0:
```python
import jax
import jax.numpy as jnp
from jax import lax
from jax.sharding import PartitionSpec as P


def entering(x, axis, combine, identity, reverse):
    size, here = (lax.axis_size(axis), lax.axis_index(axis))
    everything = jax.tree.map(lambda part: lax.all_gather(part, axis), x)
    start = jax.tree.map(
        lambda part, zero: jnp.broadcast_to(jnp.asarray(zero, part.dtype), part.shape), x, identity
    )

    def turn(k, before):
        at = size - 1 - k if reverse else k
        reached = at > here if reverse else at < here
        new = combine(before, jax.tree.map(lambda part: part[at], everything))
        return jax.tree.map(lambda a, b: jnp.where(reached, a, b), new, before)

    return lax.fori_loop(0, size, turn, start)


def spread(value, axis, source):
    kept = jnp.where(lax.axis_index(axis) == source, value, 0).astype(value.dtype)
    return lax.psum(kept, axis)


def compose(earlier, later_elem):
    highest = lax.Precision.HIGHEST
    matrix = jnp.dot(later_elem[0], earlier[0], precision=highest)
    offset = jnp.dot(later_elem[0], earlier[1], precision=highest) + later_elem[1]
    return (matrix, offset)


def shards(observations, masks, gains, transition, smoother_scale, initial_mean):
    highest = lax.Precision.HIGHEST
    state_width = transition.shape[0]
    day_count = observations.shape[0]
    observed = masks.astype(jnp.float32) * gains[None, :]
    retain = 1.0 - observed
    forcing = observed * observations
    smoother_gain = smoother_scale[:, None] * transition.T
    half_cols = state_width // lax.axis_size("pair")
    col_start = lax.axis_index("pair") * half_cols

    def forward_advance(position, product):
        scaled = jnp.dot(transition, product, precision=highest)
        return lax.dynamic_index_in_dim(retain, position, 0, False)[:, None] * scaled

    forward_half = lax.fori_loop(
        1,
        day_count,
        forward_advance,
        retain[0][:, None] * lax.dynamic_slice_in_dim(transition, col_start, half_cols, 1),
    )

    def gain_advance(position, product):
        return jnp.dot(smoother_gain, product, precision=highest)

    power_half = lax.fori_loop(
        1, day_count, gain_advance, lax.dynamic_slice_in_dim(smoother_gain, col_start, half_cols, 1)
    )
    fwd_matrix, gain_matrix = (
        lax.all_gather(forward_half, "pair", axis=1, tiled=True),
        lax.all_gather(power_half, "pair", axis=1, tiled=True),
    )

    def forward_run(mean_start):

        def forward_step(mean_prev, row_pair):
            retain_row, forcing_row = row_pair
            mean_next = retain_row * jnp.dot(transition, mean_prev, precision=highest) + forcing_row
            return (mean_next, mean_next)

        return lax.scan(forward_step, mean_start, (retain, forcing))

    def backward_run(smooth_end, means):

        def backward_step(smooth_next, mean_here):
            predicted = jnp.dot(transition, mean_here, precision=highest)
            smooth_here = mean_here + jnp.dot(
                smoother_gain, smooth_next - predicted, precision=highest
            )
            return (smooth_here, smooth_here)

        return lax.scan(backward_step, smooth_end, means, reverse=True)

    zeros_vec = jnp.zeros((state_width,), jnp.float32)
    identity = (jnp.eye(state_width, dtype=jnp.float32), zeros_vec)
    seg_count = lax.axis_size("seg")
    seg_index = lax.axis_index("seg")
    grp_count = lax.axis_size("grp")
    grp_index = lax.axis_index("grp")
    fwd_offset, unused = forward_run(zeros_vec)
    own_forward = (fwd_matrix, fwd_offset)
    before = entering(own_forward, "seg", compose, identity, False)
    through = compose(before, own_forward)
    group_total = (
        spread(through[0], "seg", seg_count - 1),
        spread(through[1], "seg", seg_count - 1),
    )
    group_before = entering(group_total, "grp", compose, identity, False)
    entry_mean = jnp.dot(group_before[0], initial_mean, precision=highest) + group_before[1]
    start_mean = jnp.dot(before[0], entry_mean, precision=highest) + before[1]
    last_mean, filtered = forward_run(start_mean)
    back_offset, unused_two = backward_run(zeros_vec, filtered)
    is_last = jnp.logical_and(seg_index == seg_count - 1, grp_index == grp_count - 1)
    boundary = jnp.dot(transition, last_mean, precision=highest)
    own_backward = (
        jnp.where(is_last, 0.0, gain_matrix),
        jnp.where(
            is_last, jnp.dot(gain_matrix, boundary, precision=highest) + back_offset, back_offset
        ),
    )
    behind = entering(own_backward, "seg", compose, identity, True)
    through_back = compose(behind, own_backward)
    back_total = (spread(through_back[0], "seg", 0), spread(through_back[1], "seg", 0))
    group_behind = entering(back_total, "grp", compose, identity, True)
    exit_smooth = group_behind[1]
    smooth_end = jnp.dot(behind[0], exit_smooth, precision=highest) + behind[1]
    smooth_end = jnp.where(is_last, boundary, smooth_end)
    unused_three, smoothed = backward_run(smooth_end, filtered)
    out_cols = state_width // lax.axis_size("pair")
    out_start = lax.axis_index("pair") * out_cols
    filtered_part = lax.dynamic_slice_in_dim(filtered, out_start, out_cols, 1)
    smoothed_part = lax.dynamic_slice_in_dim(smoothed, out_start, out_cols, 1)
    return (filtered_part, smoothed_part)


def solution(mesh):
    return jax.shard_map(
        shards,
        mesh=mesh,
        in_specs=(P(("grp", "seg"), None), P(("grp", "seg"), None), P(), P(), P(), P()),
        out_specs=(P(("grp", "seg"), "pair"), P(("grp", "seg"), "pair")),
        check_vma=False,
    )
```

profile of v0, /device:TPU:16, one launch (start us, length us, event | category | flops | bytes accessed | tf_op | source)
XLA Modules:
  0.0 1503.5 jit_solution(11549415427396379202)
XLA Ops:
  9.0 9.7 while.145
  18.7 2.1 all_gather.54
  22.0 10.7 while.149
  32.7 88.5 %all-gather.4 = f32[64,1,256]{2,1,0:T(1,128)S(1)} all-gather(f32[1,1,256]{2,1,0:T(1,128)S(1)} %bitcast.300), channel_id=3, replica_groups=mesh['seg'=64,'grp'=4,'pair'=2] {'seg'}, dimensions={0}, use_global_device_ids=true | all-gather | bytes 66560 | tf_op jit(solution)/shard_map/all_gather | solution.py:9
  122.1 96.8 %all-gather.17.cloned.1.call-done = f32[16384,256]{1,0:T(8,128)} async-done(((f32[256,256]{1,0:T(8,128)}), f32[16384,256]{1,0:T(8,128)}) %all-gather.17.cloned.1.call-update) | async-done | bytes 16777232 | tf_op jit(solution)/shard_map/all_gather | solution.py:9
  218.9 173.2 %while.150 = (s32[]{:T(128)}, f32[256,256]{1,0:T(8,128)S(1)}, f32[256]{0:T(256)S(1)}, s32[]{:T(128)}, f32[64,256,256]{2,1,0:T(8,128)}, /*index=5*/f32[64,256]{1,0:T(8,128)S(1)}, s32[]{:T(128)}, s32[]{:T(128)}) while((s32[]{:T(128)}, f32[256,256]{1,0:T(8,128)S(1)}, f32[256]{0:T(256)S(1)}, s32[]{:T(128)}, f32[64,256,256]{2,1,0:T(8,128)}, ...), condition=%wide.region_5.6_spmd.clone, body=%wide.region_4.5_spmd.clone.sunk | while | flops 202179584 | bytes 1846383 | solution.py:20
  231.1 1.3 convolution_select_fusion.8
  252.7 1.3 convolution_select_fusion.8
  260.8 1.3 convolution_select_fusion.8
  274.4 1.3 convolution_select_fusion.8
  317.7 1.3 convolution_select_fusion.8
  325.8 1.3 convolution_select_fusion.8
  339.3 1.3 convolution_select_fusion.8
  347.4 1.3 convolution_select_fusion.8
  382.6 1.3 convolution_select_fusion.8
  390.8 1.3 convolution_select_fusion.8
  392.1 2.0 fusion.30
  394.4 258.9 %all-reduce.3.cloned.1.call-done = f32[1,256,256]{2,1,0:T(8,128)} async-done(((f32[1,256,256]{2,1,0:T(8,128)}), f32[1,256,256]{2,1,0:T(8,128)}) %all-reduce.3.cloned.1.call-update) | async-done | bytes 262160 | tf_op jit(solution)/shard_map/psum | solution.py:25
  653.4 2.9 while.147
  656.3 2.0 all_gather.63
  659.5 140.2 %psum.29 = f32[1,256]{1,0:T(1,128)S(1)} all-reduce(f32[1,256]{1,0:T(1,128)S(1)} %bitcast.313), channel_id=1, replica_groups=mesh['seg'=64,'grp'=4,'pair'=2] {'seg'}, use_global_device_ids=true, to_apply=%region_7.8 | all-reduce | flops 256 | bytes 2048 | tf_op jit(solution)/shard_map/psum | solution.py:25
  799.6 7.5 all-gather.5
  807.2 10.8 while.151
  818.7 3.2 while.146
  822.5 5.4 while.152
  827.9 78.8 %all-gather.6 = f32[64,1,256]{2,1,0:T(1,128)S(1)} all-gather(f32[1,1,256]{2,1,0:T(1,128)S(1)} %bitcast.304), channel_id=5, replica_groups=mesh['seg'=64,'grp'=4,'pair'=2] {'seg'}, dimensions={0}, use_global_device_ids=true | all-gather | bytes 66560 | tf_op jit(solution)/shard_map/all_gather | solution.py:9
  906.8 174.1 %while.153 = (s32[]{:T(128)}, f32[256,256]{1,0:T(8,128)S(1)}, f32[256]{0:T(256)S(1)}, s32[]{:T(128)}, f32[64,256,256]{2,1,0:T(8,128)}, /*index=5*/f32[64,256]{1,...) while((s32[]{:T(128)}, f32[256,256]{1,0:T(8,128)S(1)}, f32[256]{0:T(256)S(1)}, ...), condition=%wide.region_17.18_spmd.clone, body=%wide.region_16.17_spmd.clone.sunk | while | flops 202179584 | bytes 1845429 | solution.py:20
  1082.0 255.0 %all-reduce.5.cloned.1.call-done = f32[1,256,256]{2,1,0:T(8,128)} async-done(((f32[1,256,256]{2,1,0:T(8,128)}), f32[1,256,256]{2,1,0:T(8,128)}) %all-reduce.5.cloned.1.call-update) | async-done | bytes 262160 | tf_op jit(solution)/shard_map/psum | solution.py:25
  1337.4 139.6 %psum.31 = f32[1,256]{1,0:T(1,128)S(1)} all-reduce(f32[1,256]{1,0:T(1,128)S(1)} %bitcast.314), channel_id=1, replica_groups=mesh['seg'=64,'grp'=4,'pair'=2] {'seg'}, use_global_device_ids=true, to_apply=%region_19.20 | all-reduce | flops 256 | bytes 2048 | tf_op jit(solution)/shard_map/psum | solution.py:25
  1477.0 7.5 all-gather.7
  1484.5 5.4 while.154
  1490.2 5.8 while.148
  (1048 shorter events, 387.1 us)
Async XLA Ops:
  7.2 810.8 %copy-start = (f32[256]{0:T(256)S(1)}, f32[256]{0:T(256)}, u32[]{:S(2)}) copy-start(f32[256]{0:T(256)} %param.31) | copy-start | bytes 3076
  7.2 387.1 %copy-start.4 = (f32[256]{0:T(256)S(1)}, f32[256]{0:T(256)}, u32[]{:S(2)}) copy-start(f32[256]{0:T(256)} %param.30) | copy-start | bytes 3076
  7.2 211.7 %all-gather.17.cloned.1.call-start = ((), (), s32[]{:S(2)}) async-start(), calls=%async_computation.4 | async-start | bytes 17039360 | tf_op jit(solution)/shard_map/all_gather | solution.py:9
  20.8 638.3 %copy-start.3 = (f32[256,256]{1,0:T(8,128)S(1)}, f32[256,256]{1,0:T(8,128)}, u32[]{:S(2)}) copy-start(f32[256,256]{1,0:T(8,128)} %all_gather.54) | copy-start | bytes 786436
  20.9 632.4 %all-reduce.3.cloned.1.call-start = ((), (), s32[]{:S(2)}) async-start(), calls=%async_computation | async-start | bytes 524288 | tf_op jit(solution)/shard_map/psum | solution.py:25
  32.7 786.0 %copy-start.1 = (f32[256,256]{1,0:T(8,128)S(1)}, f32[256,256]{1,0:T(8,128)}, u32[]{:S(2)}) copy-start(f32[256,256]{1,0:T(8,128)} %get-tuple-element.1735) | copy-start | bytes 786436
  394.2 413.0 %all-gather.13.cloned.1.call-start = ((), (), s32[]{:S(2)}) async-start(), calls=%async_computation.1 | async-start | bytes 1310720 | tf_op jit(solution)/shard_map/all_gather | solution.py:9
  653.3 253.4 %all-gather.19.cloned.1.call-start = ((), (), s32[]{:S(2)}) async-start(), calls=%async_computation.5 | async-start | bytes 17039360 | tf_op jit(solution)/shard_map/all_gather | solution.py:9
  659.0 421.8 %copy-start.2 = (f32[256,256]{1,0:T(8,128)S(1)}, f32[256,256]{1,0:T(8,128)}, u32[]{:S(2)}) copy-start(f32[256,256]{1,0:T(8,128)} %broadcast_select_fusion.5) | copy-start | bytes 786436
  659.0 678.0 %all-reduce.5.cloned.1.call-start = ((), (), s32[]{:S(2)}) async-start(), calls=%async_computation.2 | async-start | bytes 524288 | tf_op jit(solution)/shard_map/psum | solution.py:25
  1082.0 402.5 %all-gather.15.cloned.1.call-start = ((), (), s32[]{:S(2)}) async-start(), calls=%async_computation.3 | async-start | bytes 1310720 | tf_op jit(solution)/shard_map/all_gather | solution.py:9
Sparse Core Ops, SparseCore 0:
  21.0 197.8 all-gather.16
  394.3 258.9 all-reduce.2
  655.6 25.0 all-gather.12
  684.0 195.3 all-gather.18
  1082.1 254.8 all-reduce.4
  1339.0 25.0 all-gather.14
where the time goes:
time: 1510 us; the launch traced here: 1500 us
  waiting for transfers between devices  611 us (40%)
  blocking collectives  466 us (31%)
  matrix products  381 us (25%)
    psum x2, waiting for transfers between devices, spread(): return lax.psum(kept, axis)  514 us
    psum x2, blocking collectives, spread(): return lax.psum(kept, axis)  280 us
    all_gather x4, blocking collectives, entering(): everything = jax.tree.map(lambda part: lax.all_gather(part, axis), x)  182 us
    dot_general x134, matrix products, compose(): matrix = jnp.dot(later_elem[0], earlier[0], precision=highest)  179 us
    dot_general x138, matrix products, compose(): jnp.dot(later_elem[0], earlier[1], precision=highest) + later_elem[1]  167 us
    all_gather x4, waiting for transfers between devices, entering(): everything = jax.tree.map(lambda part: lax.all_gather(part, axis), x)  96.9 us
  transfers between devices with their start and end apart: 6, of which 3 were waited for; matrix products, arithmetic and copies ran while one was open for 2% of the time, Pallas kernels for 0%

commit v1 on v0

v1 whole, which is shorter than its diff:
```python
import jax
import jax.numpy as jnp
from jax import lax
from jax.experimental import pallas as pl
from jax.experimental.pallas import tpu as pltpu
from jax.sharding import PartitionSpec as P

F32 = jnp.float32
BF16 = jnp.bfloat16
M = 256
HALF = 128
DAYS = 8
XN, YN, ZN = 4, 4, 16
QN = 4
CH = 4
QD = CH * DAYS
RD = QN * QD
POWERS = 11
NROWS = HALF + 8


def split(v):
    hi = v.astype(BF16)
    return hi, (v - hi.astype(F32)).astype(BF16)


def mm(v, whi, wlo):
    rows = v.shape[0]
    hi, lo = split(v)
    both = jnp.dot(jnp.concatenate([hi, lo], 0), whi, preferred_element_type=F32)
    return both[:rows] + both[rows:] + jnp.dot(hi, wlo, preferred_element_type=F32)


def kernel(
    obs, mask, gain, trans, scale, init, filt_out, smooth_out,
    rf, athi, atlo, hp, hphi, hplo, xk, khi, klo, nb, nhi, nlo, ret4, frc4, kap,
    gin, gout, ent, fs, fb, sb, wb, vb, eb, fh, sh, frecv, srecv,
    m_send, m_recv, r_send, r_recv, k_send, k_recv, ks_send, ks_recv,
    n_send, n_recv, ns_send, ns_recv, g_send, g_recv, v_send, v_recv,
    of_send, os_send, of_recv, os_recv,
):
    seg, y, c = lax.axis_index("seg"), lax.axis_index("grp"), lax.axis_index("pair")
    x, z = lax.div(seg, ZN), lax.rem(seg, ZN)
    q, r = lax.div(z, CH), lax.rem(z, CH)
    other = 1 - c

    def at(xx, yy, zz, cc):
        return {"seg": xx * ZN + zz, "grp": yy, "pair": cc}

    def copy(src, dst, send, recv, where):
        return pltpu.make_async_remote_copy(
            src_ref=src, dst_ref=dst, send_sem=send, recv_sem=recv,
            device_id=where, device_id_type=pl.DeviceIdType.MESH,
        )

    is_master, is_worker = z == 0, r == 0
    barrier = pltpu.get_barrier_semaphore()

    def greet(where):
        pl.semaphore_signal(
            barrier, inc=1, device_id=where, device_id_type=pl.DeviceIdType.MESH
        )

    @pl.when(is_worker)
    def _():
        for k in range(1, CH):
            greet(at(x, y, z + k, c))

    @pl.when(is_master)
    def _():
        for k in range(1, QN):
            greet(at(x, y, k * CH, c))
        for k in range(1, XN * YN):
            greet(at(lax.rem(x + k % XN, XN), lax.rem(y + k // XN, YN), 0, c))
        greet(at(x, y, 0, other))

    @pl.when(jnp.logical_not(is_master))
    def _():
        greet(at(x, y, 0, c))

    observed = mask[...].astype(F32) * gain[...]
    rf[z, 0:DAYS, :] = 1.0 - observed
    rf[z, DAYS : 2 * DAYS, :] = observed * obs[...]

    @pl.when(jnp.logical_not(is_worker))
    def _():
        pl.semaphore_wait(barrier, 1)
        to_worker = copy(
            rf.at[z], rf.at[z], m_send, m_recv.at[r], at(x, y, q * CH, c)
        )
        to_worker.start()
        to_worker.wait_send()

    @pl.when(is_worker)
    def _():
        at_full = trans[...].T
        ahi, alo = split(at_full)
        athi[...] = ahi
        atlo[...] = alo
        xk[q, c] = trans[...].T[0:HALF]

        @pl.when(c == 1)
        def _():
            xk[q, c] = trans[...].T[HALF:M]

        def advance(chip, first):
            def day(j, rows):
                return mm(rows, athi[...], atlo[...]) * rf[z + chip, pl.ds(j, 1), :]

            return lax.fori_loop(first, DAYS, day, xk[q, c])

        xk[q, c] = xk[q, c] * rf[z, 0:1, :]
        xk[q, c] = advance(0, 1)
        for k in range(1, CH):
            copy(
                rf.at[z + k], rf.at[z + k], m_send, m_recv.at[k], at(x, y, 0, other)
            ).wait_recv()
            xk[q, c] = advance(k, 0)

    @pl.when(jnp.logical_and(is_worker, jnp.logical_not(is_master)))
    def _():
        pl.semaphore_wait(barrier, 1)
        days_to = copy(
            rf.at[pl.ds(z, CH)], rf.at[pl.ds(z, CH)], r_send, r_recv.at[q], at(x, y, 0, c)
        )
        days_to.start()
        map_to = copy(xk.at[q, c], xk.at[q, c], k_send, k_recv.at[q], at(x, y, 0, c))
        map_to.start()
        days_to.wait_send()
        map_to.wait_send()

    @pl.when(is_master)
    def _():
        pl.semaphore_wait(barrier, ZN - 1 + XN * YN - 1 + 1)

        def to_sibling(qq):
            return copy(
                xk.at[qq, c], xk.at[qq, c], ks_send.at[qq], ks_recv.at[qq], at(x, y, 0, other)
            )

        to_sibling(0).start()

        h0 = trans[...] * scale[...]
        hp[...] = h0
        hphi[0], hplo[0] = split(h0)

        def square(k, _):
            h = hp[...]
            h = jnp.dot(h, h, precision=lax.Precision.HIGHEST, preferred_element_type=F32)
            hp[...] = h
            hphi[k], hplo[k] = split(h)
            return 0

        lax.fori_loop(1, POWERS, square, 0)

        for k in range(1, QN):
            copy(
                rf.at[pl.ds(k * CH, CH)], rf.at[pl.ds(k * CH, CH)], r_send, r_recv.at[k],
                at(x, y, 0, other),
            ).wait_recv()
        ret4[...] = jnp.zeros_like(ret4)
        frc4[...] = jnp.zeros_like(frc4)

        for qq in range(QN):
            for k in range(CH):
                ret4[k * DAYS : (k + 1) * DAYS, qq, :] = rf[qq * CH + k, 0:DAYS, :]
                frc4[k * DAYS : (k + 1) * DAYS, qq, :] = rf[qq * CH + k, DAYS : 2 * DAYS, :]

        def day4(j, rows):
            return mm(rows, athi[...], atlo[...]) * ret4[j] + frc4[j]

        kap[...] = lax.fori_loop(0, QD, day4, jnp.zeros((8, M), F32))

        for k in range(1, QN):
            copy(
                xk.at[k, c], xk.at[k, c], k_send, k_recv.at[k], at(x, y, 0, other)
            ).wait_recv()
            to_sibling(k).start()
        rows = jnp.concatenate(
            [xk[0, c], jnp.broadcast_to(kap[0:1, :], (8, M))], 0
        )
        sub = lax.broadcasted_iota(jnp.int32, (NROWS, M), 0)
        for k in range(QN):
            to_sibling(k).wait_recv()
            for half in range(2):
                khi[k, half * HALF : (half + 1) * HALF, :], klo[
                    k, half * HALF : (half + 1) * HALF, :
                ] = split(xk[k, half])
            if k:
                rows = mm(rows, khi[k], klo[k]) + jnp.where(sub < HALF, 0.0, kap[k : k + 1, :])
        nb[x, c] = rows

        def to_peer(d):
            return copy(
                nb.at[x, c], nb.at[x, c], n_send.at[d], n_recv.at[x],
                at(lax.rem(x + d, XN), y, 0, c),
            )

        def share(xs):
            return copy(
                nb.at[xs, c], nb.at[xs, c], ns_send.at[xs], ns_recv.at[xs], at(x, y, 0, other)
            )

        for d in (2, 1, 3):
            to_peer(d).start()
        share(x).start()
        for d in (1, 3, 2):
            xs = lax.rem(x + d, XN)
            copy(
                nb.at[xs, c], nb.at[xs, c], n_send.at[d], n_recv.at[xs], at(x, y, 0, other)
            ).wait_recv()
            share(xs).start()
        for xs in range(XN):
            share(xs).wait_recv()
            for half in range(2):
                nhi[xs, half * HALF : (half + 1) * HALF, :], nlo[
                    xs, half * HALF : (half + 1) * HALF, :
                ] = split(nb[xs, half, 0:HALF, :])

        @pl.when(y == 0)
        def _():
            gin[...] = jnp.broadcast_to(init[...], (8, M))

        @pl.when(y > 0)
        def _():
            copy(gin, gin, g_send, g_recv, at(x, y, 0, other)).wait_recv()

        state = gin[...]
        for k in range(XN):
            ent[k] = state
            state = mm(state, nhi[k], nlo[k]) + nb[k, 0, HALF : HALF + 1, :]
        gout[...] = state

        def to_group():
            return copy(gout, gin, g_send, g_recv, at(x, lax.rem(y + 1, YN), 0, c))

        @pl.when(y < YN - 1)
        def _():
            to_group().start()

        state = ent[x]
        fs[...] = jnp.zeros_like(fs)
        for k in range(QN):
            fs[k : k + 1, :] = state[0:1, :]
            if k < QN - 1:
                state = mm(state, khi[k], klo[k]) + kap[k : k + 1, :]

        def run4(j, rows):
            rows = day4(j, rows)
            for k in range(QN):
                fb[pl.ds(k * QD + j, 1), :] = rows[k : k + 1, :]
            return rows

        last = lax.fori_loop(0, QD, run4, fs[...])

        def out_copy(src, dst, send, recv, k):
            zz = k
            return copy(src.at[pl.ds(zz * DAYS, DAYS)], dst, send.at[k], recv, at(x, y, zz, c))

        @pl.when(c == 0)
        def _():
            fh[...] = fb[:, 0:HALF]

        @pl.when(c == 1)
        def _():
            fh[...] = fb[:, HALF:M]

        order = (8, 7, 9, 6, 10, 5, 11, 4, 12, 3, 13, 2, 14, 1, 15)
        for k in order:
            out_copy(fh, frecv, of_send, of_recv, k).start()
        filt_out[...] = fh[0:DAYS, :]

        weight = 1.0 - scale[...] * jnp.sum(trans[...] * trans[...], axis=0, keepdims=True)
        sb[0:RD, :] = fb[...] * weight
        sb[RD : RD + HALF // 2, :] = jnp.zeros((HALF // 2, M), F32)
        for k in range(7):
            sb[0:RD, :] = sb[0:RD, :] + mm(sb[1 << k : (1 << k) + RD, :], hphi[k], hplo[k])
        me = y * XN + x
        boundary = mm(jnp.broadcast_to(last[QN - 1 : QN, :], (8, M)), athi[...], atlo[...])
        sub8 = lax.broadcasted_iota(jnp.int32, (8, M), 0)
        vb[me] = jnp.where(sub8 == 0, sb[0:1, :], boundary)

        def to_plane(k):
            return copy(
                vb.at[me], vb.at[me], v_send.at[k], v_recv.at[me],
                at(lax.rem(x + k % XN, XN), lax.rem(y + k // XN, YN), 0, c),
            )

        plane = (10, 2, 8, 6, 9, 11, 14, 5, 7, 13, 15, 1, 3, 4, 12)
        for k in plane:
            to_plane(k).start()
        for k in plane:
            src = lax.rem(y + k // XN, YN) * XN + lax.rem(x + k % XN, XN)
            copy(
                vb.at[src], vb.at[src], v_send.at[k], v_recv.at[src], at(x, y, 0, other)
            ).wait_recv()

        eb[...] = jnp.zeros_like(eb)
        for k in range(1, XN * YN):
            eb[k - 1 : k, :] = vb[k, 0:1, :]
        eb[XN * YN - 1 : XN * YN, :] = vb[XN * YN - 1, 1:2, :]
        for k in range(4):
            eb[0:16, :] = eb[0:16, :] + mm(eb[1 << k : (1 << k) + 16, :], hphi[7 + k], hplo[7 + k])

        wb[RD - 8 : RD, :] = jnp.zeros((8, M), F32)
        wb[RD - 1 : RD, :] = mm(jnp.broadcast_to(eb[pl.ds(me, 1), :], (8, M)), hphi[0], hplo[0])[0:1, :]
        for k in range(7):
            n = 1 << k
            wb[RD - 2 * n : RD - n, :] = mm(
                wb[RD - max(n, 8) : RD, :], hphi[k], hplo[k]
            )[max(n, 8) - n : max(n, 8), :]
        total = sb[0:RD, :] + wb[...]

        @pl.when(c == 0)
        def _():
            sh[...] = total[:, 0:HALF]

        @pl.when(c == 1)
        def _():
            sh[...] = total[:, HALF:M]

        for k in order:
            out_copy(sh, srecv, os_send, os_recv, k).start()
        smooth_out[...] = sh[0:DAYS, :]

        for k in range(QN):
            to_sibling(k).wait_send()
        for d in range(1, XN):
            to_peer(d).wait_send()
        for xs in range(XN):
            share(xs).wait_send()

        @pl.when(y < YN - 1)
        def _():
            to_group().wait_send()

        for k in plane:
            to_plane(k).wait_send()
        for k in order:
            out_copy(fh, frecv, of_send, of_recv, k).wait_send()
            out_copy(sh, srecv, os_send, os_recv, k).wait_send()

    @pl.when(jnp.logical_not(is_master))
    def _():
        copy(frecv, frecv, r_send, of_recv, at(x, y, 0, c)).wait_recv()
        filt_out[...] = frecv[...]
        copy(srecv, srecv, r_send, os_recv, at(x, y, 0, c)).wait_recv()
        smooth_out[...] = srecv[...]


def shards(observations, masks, gains, transition, smoother_scale, initial_mean):
    vmem = pl.BlockSpec(memory_space=pltpu.VMEM)
    dma = pltpu.SemaphoreType.DMA

    def buf(*shape, dtype=F32):
        return pltpu.VMEM(shape, dtype)

    out = jax.ShapeDtypeStruct((DAYS, HALF), F32)
    return pl.pallas_call(
        kernel,
        out_shape=(out, out),
        in_specs=[vmem] * 6,
        out_specs=(vmem, vmem),
        scratch_shapes=[
            buf(ZN, 2 * DAYS, M),
            buf(M, M, dtype=BF16), buf(M, M, dtype=BF16),
            buf(M, M), buf(POWERS, M, M, dtype=BF16), buf(POWERS, M, M, dtype=BF16),
            buf(QN, 2, HALF, M), buf(QN, M, M, dtype=BF16), buf(QN, M, M, dtype=BF16),
            buf(XN, 2, NROWS, M), buf(XN, M, M, dtype=BF16), buf(XN, M, M, dtype=BF16),
            buf(QD, 8, M), buf(QD, 8, M), buf(8, M),
            buf(8, M), buf(8, M), buf(XN, 8, M),
            buf(8, M), buf(RD, M), buf(RD + HALF // 2, M), buf(RD, M),
            buf(XN * YN, 8, M), buf(32, M),
            buf(RD, HALF), buf(RD, HALF), buf(DAYS, HALF), buf(DAYS, HALF),
            dma, dma((CH,)), dma, dma((QN,)), dma, dma((QN,)), dma((QN,)), dma((QN,)),
            dma((XN,)), dma((XN,)), dma((XN,)), dma((XN,)), dma, dma,
            dma((XN * YN,)), dma((XN * YN,)),
            dma((ZN,)), dma((ZN,)), dma, dma,
        ],
        compiler_params=pltpu.CompilerParams(
            collective_id=0, has_side_effects=True, vmem_limit_bytes=48 * 2**20
        ),
        name="smoother",
    )(
        observations, masks, gains.reshape(1, M), transition,
        smoother_scale.reshape(1, M), initial_mean.reshape(1, M),
    )


def solution(mesh):
    return jax.shard_map(
        shards,
        mesh=mesh,
        in_specs=(P(("grp", "seg"), None), P(("grp", "seg"), None), P(), P(), P(), P()),
        out_specs=(P(("grp", "seg"), "pair"), P(("grp", "seg"), "pair")),
        check_vma=False,
    )
```

time: 1510 us -> 74.9 us (0.05)
  the two profiles are of different devices: /device:TPU:16 before, /device:TPU:32 now
where the time goes in v1:
time: 74.9 us; the launch traced here: 74.6 us
  Pallas kernels  69.8 us (93%)
  local copies, waits for them, and re-layouts  4.22 us (6%)
    pallas_call x1, Pallas kernels, shards(): pl.pallas_call(kernel, out_shape=(out, out), in_specs=[vmem] * 6, out_spe...  69.8 us
    unnamed x14, local copies, waits for them, and re-layouts  4.22 us

profile of v1, /device:TPU:32, one launch (start us, length us, event | category | flops | bytes accessed | tf_op | source)
XLA Modules:
  0.0 74.6 jit_solution(12388172549526971657)
XLA Ops:
  0.6 0.0 copy-start.4
  0.6 0.0 copy-start.5
  0.7 0.0 copy-start.3
  0.7 0.7 copy-done.4
  1.3 0.0 copy-done.5
  1.3 0.0 copy-done.3
  1.3 0.0 copy-start
  1.3 0.9 %copy-done = f32[256,256]{1,0:T(8,128)S(1)} copy-done((f32[256,256]{1,0:T(8,128)S(1)}, f32[256,256]{1,0:T(8,128)}, u32[]{:S(2)}) %copy-start) | copy-done | bytes 262168
  2.3 0.0 copy-start.1
  2.3 0.7 copy-done.1
  3.0 0.0 copy-start.2
  3.0 0.7 copy-done.2
  3.7 69.8 %smoother.1 = (f32[8,128]{1,0:T(8,128)S(1)}, f32[8,128]{1,0:T(8,128)S(1)}) custom-call(f32[8,256]{1,0:T(8,128)S(1)} %copy-done.1, s32[8,256]{1,0:T(8,128)S(1)} %copy-done.2, f32[1,256]{1,0:T(1,128)S(1)} %bitcast.3, f32[256,256]{1,0:T(8,128)S(1)} %copy-done, f32[1,256]{1,0:T(1,128)S(1)} %bitcast.4, f32[1,256]{1,0:T(1,128)S(1)} %bitcast.5), custom_call_target="tpu_custom_call" | custom-call | tf_op jit(solution)/shard_map/smoother/pallas_call | solution.py:359
  73.5 0.6 copy.10
  74.1 0.6 copy.11
Async XLA Ops:
  0.6 0.7 copy-start.4
  0.6 0.7 copy-start.5
  0.7 0.7 copy-start.3
  1.3 0.9 %copy-start = (f32[256,256]{1,0:T(8,128)S(1)}, f32[256,256]{1,0:T(8,128)}, u32[]{:S(2)}) copy-start(f32[256,256]{1,0:T(8,128)} %trans.1) | copy-start | bytes 786436
  2.3 0.7 copy-start.1
  3.0 0.7 copy-start.2

commit v2 on v1

v2 whole, which is shorter than its diff:
```python
import jax
import jax.numpy as jnp
from jax import lax
from jax.experimental import pallas as pl
from jax.experimental.pallas import tpu as pltpu
from jax.sharding import PartitionSpec as P

F32 = jnp.float32
BF16 = jnp.bfloat16
M = 256
HALF = 128
DAYS = 8
XN, YN, ZN = 4, 4, 16
QN = 4
CH = 4
QD = CH * DAYS
RINGS = XN * YN
POWERS = 11
ROWS = HALF + 8


def split(v):
    hi = v.astype(BF16)
    return hi, (v - hi.astype(F32)).astype(BF16)


def mm(v, whi, wlo):
    rows = v.shape[0]
    if rows % 16 == 8 and rows > 8:
        return jnp.concatenate([mm(v[: rows - 8], whi, wlo), mm(v[rows - 8 :], whi, wlo)], 0)
    hi, lo = split(v)
    both = jnp.dot(jnp.concatenate([hi, lo], 0), whi, preferred_element_type=F32)
    return both[:rows] + both[rows:] + jnp.dot(hi, wlo, preferred_element_type=F32)


def plus_offset(rows, offset):
    n = rows.shape[0] - rows.shape[0] % HALF
    return jnp.concatenate([rows[:n], rows[n:] + offset], 0)


def whole(halves):
    return jnp.concatenate([halves[0, 0:HALF, :], halves[1, 0:HALF, :], halves[0, HALF:ROWS, :]], 0)


def kernel(
    obs_hbm, mask_hbm, gain_hbm, trans_hbm, scale_hbm, init_hbm, filt_out, smooth_out,
    obs, mask, gain, trans, scale, init,
    rf, atf, athi, atlo, hp, hphi, hplo, xt, mk, khi, klo, mv, vo, vhi, vlo, sm, tm, pre, thi, tlo, pc, phi, plo,
    nb, nhi, nlo, ret4, frc4, gin, gout, ent, st, fs, fb, sb, wb, vb, eb,
    fh, sh, frecv, srecv,
    in_sem, m_send, m_recv, k_send, k_recv, ks_send, ks_recv, w_send, w_recv, ws_send, ws_recv,
    p_send, p_recv, n_send, n_recv, ns_send, ns_recv, g_send, g_recv, v_send, v_recv,
    of_send, os_send, of_recv, os_recv,
):
    seg, y, c = lax.axis_index("seg"), lax.axis_index("grp"), lax.axis_index("pair")
    x, z = lax.div(seg, ZN), lax.rem(seg, ZN)
    q, r = lax.div(z, CH), lax.rem(z, CH)
    other = 1 - c
    is_worker = r == 0

    fetches = [
        pltpu.make_async_copy(src, dst, in_sem.at[k])
        for k, (src, dst) in enumerate(
            (
                (mask_hbm, mask), (obs_hbm, obs), (gain_hbm, gain),
                (trans_hbm, trans), (scale_hbm, scale), (init_hbm, init),
            )
        )
    ]
    for fetch in fetches:
        fetch.start()

    def at(xx, yy, zz, cc):
        return {"seg": xx * ZN + zz, "grp": yy, "pair": cc}

    sibling = at(x, y, z, other)

    def copy(src, dst, send, recv, where):
        return pltpu.make_async_remote_copy(
            src_ref=src, dst_ref=dst, send_sem=send, recv_sem=recv,
            device_id=where, device_id_type=pl.DeviceIdType.MESH,
        )

    def arrival(dst, send, recv):
        return copy(dst, dst, send, recv, sibling)

    barrier = pltpu.get_barrier_semaphore()

    def greet(where):
        pl.semaphore_signal(
            barrier, inc=1, device_id=where, device_id_type=pl.DeviceIdType.MESH
        )

    def ring_peer(d):
        return at(x, y, lax.rem(q + d, QN) * CH, c)

    def plane_peer(k):
        return at(lax.rem(x + k % XN, XN), lax.rem(y + k // XN, YN), z, c)

    @pl.when(is_worker)
    def _():
        for k in range(1, CH):
            greet(at(x, y, z + k, c))
        for k in range(1, QN):
            greet(ring_peer(k))
        for k in range(1, RINGS):
            greet(plane_peer(k))
        greet(sibling)

    @pl.when(jnp.logical_not(is_worker))
    def _():
        greet(at(x, y, q * CH, c))

    for fetch in fetches[:3]:
        fetch.wait()
    observed = mask[...].astype(F32) * gain[...]
    rf[r, 0:DAYS, :] = 1.0 - observed
    rf[r, DAYS : 2 * DAYS, :] = observed * obs[...]

    @pl.when(jnp.logical_not(is_worker))
    def _():
        pl.semaphore_wait(barrier, 1)
        to_worker = copy(rf.at[r], rf.at[r], m_send, m_recv.at[r], at(x, y, q * CH, c))
        to_worker.start()
        for fetch in fetches[3:]:
            fetch.wait()
        to_worker.wait_send()
        arrival(frecv, m_send, of_recv).wait_recv()
        filt_out[...] = frecv[...]
        arrival(srecv, m_send, os_recv).wait_recv()
        smooth_out[...] = srecv[...]

    @pl.when(is_worker)
    def _():
        for fetch in fetches[3:]:
            fetch.wait()

        at_full = trans[...].T
        atf[...] = at_full
        athi[...], atlo[...] = split(at_full)
        h0 = trans[...] * scale[...]
        hp[...] = h0
        hphi[0], hplo[0] = split(h0)

        def advance(chip, first, rows):
            def day(j, rows):
                rows = plus_offset(
                    mm(rows, athi[...], atlo[...]) * rf[chip, pl.ds(j, 1), :],
                    rf[chip, pl.ds(DAYS + j, 1), :],
                )
                xt[chip * DAYS + j] = rows
                return rows

            return lax.fori_loop(first, DAYS, day, rows)

        rows = jnp.concatenate(
            [
                atf[pl.ds(pl.multiple_of(c * HALF, HALF), HALF), :] * rf[0, 0:1, :],
                jnp.broadcast_to(rf[0, DAYS : DAYS + 1, :], (8, M)),
            ],
            0,
        )
        xt[0] = rows
        rows = advance(0, 1, rows)
        for k in range(1, CH):
            arrival(rf.at[k], m_send, m_recv.at[k]).wait_recv()
            rows = advance(k, 0, rows)
        mk[q, c] = rows

        pl.semaphore_wait(barrier, CH - 1 + QN - 1 + RINGS - 1 + 1)

        def ring_send(buf, send, recv, d):
            return copy(buf.at[q, c], buf.at[q, c], send.at[d], recv.at[q], ring_peer(d))

        def ring_share(buf, send, recv, k):
            return copy(buf.at[k, c], buf.at[k, c], send.at[k], recv.at[k], sibling)

        for d in (2, 1, 3):
            ring_send(mk, k_send, k_recv, d).start()
        ring_share(mk, ks_send, ks_recv, q).start()

        def chunk_share(k):
            return copy(xt.at[k * DAYS - 1], pc.at[k - 1], p_send.at[k - 1], p_recv.at[k - 1], sibling)

        for k in range(1, CH):
            chunk_share(k).start()

        weight = 1.0 - scale[...] * jnp.sum(trans[...] * trans[...], axis=0, keepdims=True)

        def back(k, rows):
            return xt[QD - 2 - k] * weight + mm(rows, hphi[0], hplo[0])

        mv[q, c] = lax.fori_loop(0, QD - 1, back, xt[QD - 1] * weight)

        for d in (1, 3, 2):
            k = lax.rem(q + d, QN)
            arrival(mk.at[k, c], k_send.at[d], k_recv.at[k]).wait_recv()
            ring_share(mk, ks_send, ks_recv, k).start()
        for d in (2, 1, 3):
            ring_send(mv, w_send, w_recv, d).start()
        ring_share(mv, ws_send, ws_recv, q).start()
        for k in range(QN):
            ring_share(mk, ks_send, ks_recv, k).wait_recv()
            for half in range(2):
                part = slice(half * HALF, (half + 1) * HALF)
                khi[k, part, :], klo[k, part, :] = split(mk[k, half, 0:HALF, :])
        rows = mk[0, c]
        for k in range(1, QN):
            rows = plus_offset(mm(rows, khi[k], klo[k]), mk[k, 0, HALF : HALF + 1, :])
        nb[x, c] = rows

        def to_peer(d):
            return copy(
                nb.at[x, c], nb.at[x, c], n_send.at[d], n_recv.at[x],
                at(lax.rem(x + d, XN), y, z, c),
            )

        def share(xs):
            return copy(nb.at[xs, c], nb.at[xs, c], ns_send.at[xs], ns_recv.at[xs], sibling)

        for d in (2, 1, 3):
            to_peer(d).start()
        share(x).start()

        def square(k, _):
            h = hp[...]
            h = jnp.dot(h, h, precision=lax.Precision.HIGHEST, preferred_element_type=F32)
            hp[...] = h
            hphi[k], hplo[k] = split(h)
            return 0

        lax.fori_loop(1, POWERS, square, 0)
        ret4[...] = jnp.zeros_like(ret4)
        frc4[...] = jnp.zeros_like(frc4)
        for k in range(CH):
            ret4[:, k, :] = rf[k, 0:DAYS, :]
            frc4[:, k, :] = rf[k, DAYS : 2 * DAYS, :]
        for k in range(1, CH):
            arrival(pc.at[k - 1], p_send.at[k - 1], p_recv.at[k - 1]).wait_recv()
            mine, theirs = split(xt[k * DAYS - 1, 0:HALF, :]), split(pc[k - 1, 0:HALF, :])
            own = pl.ds(pl.multiple_of(c * HALF, HALF), HALF)
            far = pl.ds(pl.multiple_of(other * HALF, HALF), HALF)
            phi[k - 1, own, :], plo[k - 1, own, :] = mine
            phi[k - 1, far, :], plo[k - 1, far, :] = theirs
        for d in (1, 3, 2):
            xs = lax.rem(x + d, XN)
            arrival(nb.at[xs, c], n_send.at[d], n_recv.at[xs]).wait_recv()
            share(xs).start()
        for xs in range(XN):
            share(xs).wait_recv()
            for half in range(2):
                part = slice(half * HALF, (half + 1) * HALF)
                nhi[xs, part, :], nlo[xs, part, :] = split(nb[xs, half, 0:HALF, :])

        def smoother_map():
            for d in (1, 3, 2):
                k = lax.rem(q + d, QN)
                arrival(mv.at[k, c], w_send.at[d], w_recv.at[k]).wait_recv()
                ring_share(mv, ws_send, ws_recv, k).start()
            for k in range(QN):
                ring_share(mv, ws_send, ws_recv, k).wait_recv()
            sm[...] = whole(mv[QN - 1])
            for k in (2, 1, 0):

                @pl.when(q == k)
                def _():
                    vhi[1], vlo[1] = split(sm[0:M, :])
                    vo[1] = sm[M : M + 8, :]

                later = mm(sm[...], hphi[5], hplo[5])
                lhi, llo = split(later[:M])
                sm[...] = (
                    plus_offset(mm(whole(mk[k]), lhi, llo), later[M:]) + whole(mv[k])
                )
            vhi[0], vlo[0] = split(sm[0:M, :])
            vo[0] = sm[M : M + 8, :]

        def group_map():
            tm[...] = whole(nb[0])
            for k in range(1, XN):

                @pl.when(x == k)
                def _():
                    pre[...] = tm[...]

                tm[...] = plus_offset(mm(tm[...], nhi[k], nlo[k]), nb[k, 0, HALF : HALF + 1, :])
            thi[0], tlo[0] = split(tm[0:M, :])
            thi[1], tlo[1] = split(pre[0:M, :])

        def to_group():
            return copy(gout, gin, g_send, g_recv, at(x, lax.rem(y + 1, YN), z, c))

        @pl.when(y == 0)
        def _():
            state = jnp.broadcast_to(init[...], (8, M))
            for k in range(XN):
                ent[k] = state
                state = mm(state, nhi[k], nlo[k]) + nb[k, 0, HALF : HALF + 1, :]
            gout[...] = state
            to_group().start()
            st[0] = ent[x]

        @pl.when(y > 0)
        def _():
            group_map()

        @pl.when(y > 1)
        def _():
            smoother_map()

        @pl.when(y > 0)
        def _():
            arrival(gin, g_send, g_recv).wait_recv()
            gout[...] = mm(gin[...], thi[0], tlo[0]) + tm[M : M + 1, :]

            @pl.when(y < YN - 1)
            def _():
                to_group().start()

            st[0] = jnp.where(
                x == 0, gin[...], mm(gin[...], thi[1], tlo[1]) + pre[M : M + 1, :]
            )

        @pl.when(y < 2)
        def _():
            smoother_map()

        v = (mm(st[0], vhi[0], vlo[0]) + vo[0, 0:1, :])[0:1, :]
        boundary = mm(gout[...], athi[...], atlo[...])
        me = y * XN + x
        sub8 = lax.broadcasted_iota(jnp.int32, (8, M), 0)
        vb[me] = jnp.where(sub8 == 0, v, boundary)

        def to_plane(k):
            return copy(vb.at[me], vb.at[me], v_send.at[k], v_recv.at[me], plane_peer(k))

        plane = (10, 2, 8, 6, 9, 11, 14, 5, 7, 13, 15, 1, 3, 4, 12)
        for k in plane:
            to_plane(k).start()

        for k in range(1, QN):
            st[k] = mm(st[k - 1], khi[k - 1], klo[k - 1]) + mk[k - 1, 0, HALF : HALF + 1, :]
        state = st[q]
        after = mm(st[lax.min(q + 1, QN - 1)], vhi[1], vlo[1]) + vo[1, 0:1, :]
        fs[...] = jnp.zeros_like(fs)
        fs[0:1, :] = state[0:1, :]
        for k in range(1, CH):
            fs[k : k + 1, :] = (
                mm(state, phi[k - 1], plo[k - 1]) + pc[k - 1, HALF : HALF + 1, :]
            )[0:1, :]
        days = fs[...]
        for j in range(DAYS):
            days = mm(days, athi[...], atlo[...]) * ret4[j] + frc4[j]
            for k in range(CH):
                fb[k * DAYS + j : k * DAYS + j + 1, :] = days[k : k + 1, :]

        @pl.when(c == 0)
        def _():
            fh[...] = fb[:, 0:HALF]

        @pl.when(c == 1)
        def _():
            fh[...] = fb[:, HALF:M]

        def out_copy(src, dst, send, recv, k):
            return copy(
                src.at[pl.ds(k * DAYS, DAYS)], dst, send.at[k], recv, at(x, y, z + k, c)
            )

        for k in (3, 2, 1):
            out_copy(fh, frecv, of_send, of_recv, k).start()
        filt_out[...] = fh[0:DAYS, :]

        sb[0:QD, :] = fb[...] * weight
        sb[QD : 2 * QD, :] = jnp.zeros((QD, M), F32)
        for k in range(5):
            sb[0:QD, :] = sb[0:QD, :] + mm(sb[1 << k : (1 << k) + QD, :], hphi[k], hplo[k])

        eb[...] = jnp.zeros_like(eb)
        for k in plane:
            src = lax.rem(y + k // XN, YN) * XN + lax.rem(x + k % XN, XN)
            arrival(vb.at[src], v_send.at[k], v_recv.at[src]).wait_recv()
        for k in range(1, RINGS):
            eb[k - 1 : k, :] = vb[k, 0:1, :]
        eb[RINGS - 1 : RINGS, :] = vb[RINGS - 1, 1:2, :]
        for k in range(4):
            eb[0:16, :] = eb[0:16, :] + mm(eb[1 << k : (1 << k) + 16, :], hphi[7 + k], hplo[7 + k])
        behind = jnp.broadcast_to(eb[pl.ds(me, 1), :], (8, M))
        left = QN - 1 - q
        behind = jnp.where(lax.rem(left, 2) == 1, mm(behind, hphi[5], hplo[5]), behind)
        behind = jnp.where(left >= 2, mm(behind, hphi[6], hplo[6]), behind)
        behind = jnp.where(left > 0, behind + after, behind)

        wb[QD - 8 : QD, :] = jnp.zeros((8, M), F32)
        wb[QD - 1 : QD, :] = mm(behind, hphi[0], hplo[0])[0:1, :]
        for k in range(5):
            n = 1 << k
            m = max(n, 8)
            wb[QD - 2 * n : QD - n, :] = mm(wb[QD - m : QD, :], hphi[k], hplo[k])[m - n : m, :]
        total = sb[0:QD, :] + wb[...]

        @pl.when(c == 0)
        def _():
            sh[...] = total[:, 0:HALF]

        @pl.when(c == 1)
        def _():
            sh[...] = total[:, HALF:M]

        for k in (3, 2, 1):
            out_copy(sh, srecv, os_send, os_recv, k).start()
        smooth_out[...] = sh[0:DAYS, :]

        for d in range(1, QN):
            ring_send(mk, k_send, k_recv, d).wait_send()
            ring_send(mv, w_send, w_recv, d).wait_send()
            chunk_share(d).wait_send()
        for k in range(QN):
            ring_share(mk, ks_send, ks_recv, k).wait_send()
            ring_share(mv, ws_send, ws_recv, k).wait_send()
        for d in range(1, XN):
            to_peer(d).wait_send()
        for xs in range(XN):
            share(xs).wait_send()

        @pl.when(y < YN - 1)
        def _():
            to_group().wait_send()

        for k in plane:
            to_plane(k).wait_send()
        for k in (3, 2, 1):
            out_copy(fh, frecv, of_send, of_recv, k).wait_send()
            out_copy(sh, srecv, os_send, os_recv, k).wait_send()


def shards(observations, masks, gains, transition, smoother_scale, initial_mean):
    hbm, vmem = pl.BlockSpec(memory_space=pltpu.HBM), pl.BlockSpec(memory_space=pltpu.VMEM)
    dma = pltpu.SemaphoreType.DMA

    def buf(*shape, dtype=F32):
        return pltpu.VMEM(shape, dtype)

    def halves(*shape):
        return [buf(*shape, dtype=BF16), buf(*shape, dtype=BF16)]

    out = jax.ShapeDtypeStruct((DAYS, HALF), F32)
    return pl.pallas_call(
        kernel,
        out_shape=(out, out),
        in_specs=[hbm] * 6,
        out_specs=(vmem, vmem),
        scratch_shapes=[
            buf(DAYS, M), buf(DAYS, M, dtype=jnp.int32), buf(1, M), buf(M, M), buf(1, M), buf(1, M),
            buf(CH, 2 * DAYS, M), buf(M, M), *halves(M, M),
            buf(M, M), *halves(POWERS, M, M),
            buf(QD, ROWS, M),
            buf(QN, 2, ROWS, M), *halves(QN, M, M),
            buf(QN, 2, ROWS, M), buf(2, 8, M), *halves(2, M, M),
            buf(M + 8, M), buf(M + 8, M), buf(M + 8, M), *halves(2, M, M),
            buf(CH - 1, ROWS, M), *halves(CH - 1, M, M),
            buf(XN, 2, ROWS, M), *halves(XN, M, M),
            buf(DAYS, 8, M), buf(DAYS, 8, M),
            buf(8, M), buf(8, M), buf(XN, 8, M), buf(QN, 8, M),
            buf(8, M), buf(QD, M), buf(2 * QD, M), buf(QD, M),
            buf(RINGS, 8, M), buf(32, M),
            buf(QD, HALF), buf(QD, HALF), buf(DAYS, HALF), buf(DAYS, HALF),
            dma((6,)), dma, dma((CH,)),
            dma((QN,)), dma((QN,)), dma((QN,)), dma((QN,)),
            dma((QN,)), dma((QN,)), dma((QN,)), dma((QN,)),
            dma((CH,)), dma((CH,)),
            dma((XN,)), dma((XN,)), dma((XN,)), dma((XN,)),
            dma, dma, dma((RINGS,)), dma((RINGS,)),
            dma((CH,)), dma((CH,)), dma, dma,
        ],
        compiler_params=pltpu.CompilerParams(
            collective_id=0, has_side_effects=True, vmem_limit_bytes=48 * 2**20
        ),
        name="smoother",
    )(
        observations, masks, gains.reshape(1, M), transition,
        smoother_scale.reshape(1, M), initial_mean.reshape(1, M),
    )


def solution(mesh):
    return jax.shard_map(
        shards,
        mesh=mesh,
        in_specs=(P(("grp", "seg"), None), P(("grp", "seg"), None), P(), P(), P(), P()),
        out_specs=(P(("grp", "seg"), "pair"), P(("grp", "seg"), "pair")),
        check_vma=False,
    )
```

time: 74.9 us -> 65.6 us (0.88)
  Pallas kernels: 69.8 us -> 60.4 us
    pallas_call x1, Pallas kernels: 69.8 us -> 60.4 us  [shards(): pl.pallas_call(kernel, out_shape=(out, out), in_specs=[hbm] * 6, out_spec...]
where the time goes in v2:
time: 65.6 us; the launch traced here: 65.3 us
  Pallas kernels  60.4 us (92%)
  local copies, waits for them, and re-layouts  4.22 us (6%)
  between operations  0.67 us (1%)
    pallas_call x1, Pallas kernels, shards(): pl.pallas_call(kernel, out_shape=(out, out), in_specs=[hbm] * 6, out_spec...  60.4 us
    unnamed x14, local copies, waits for them, and re-layouts  4.22 us

profile of v2, /device:TPU:32, one launch (start us, length us, event | category | flops | bytes accessed | tf_op | source)
XLA Modules:
  0.0 65.3 jit_solution(14694714898121263787)
XLA Ops:
  0.6 0.0 copy-start.4
  0.6 0.0 copy-start.5
  0.7 0.0 copy-start.3
  0.7 0.7 copy-done.4
  1.3 0.0 copy-done.5
  1.3 0.0 copy-done.3
  1.3 0.0 copy-start
  1.3 0.9 %copy-done = f32[256,256]{1,0:T(8,128)S(1)} copy-done((f32[256,256]{1,0:T(8,128)S(1)}, f32[256,256]{1,0:T(8,128)}, u32[]{:S(2)}) %copy-start) | copy-done | bytes 262168
  2.3 0.0 copy-start.1
  2.3 0.7 %copy-done.1 = f32[8,256]{1,0:T(8,128)S(1)} copy-done((f32[8,256]{1,0:T(8,128)S(1)}, f32[8,256]{1,0:T(8,128)}, u32[]{:S(2)}) %copy-start.1) | copy-done | bytes 8216
  3.0 0.0 copy-start.2
  3.0 0.7 %copy-done.2 = s32[8,256]{1,0:T(8,128)S(1)} copy-done((s32[8,256]{1,0:T(8,128)S(1)}, s32[8,256]{1,0:T(8,128)}, u32[]{:S(2)}) %copy-start.2) | copy-done | bytes 8216
  3.7 60.4 %smoother.1 = (f32[8,128]{1,0:T(8,128)S(1)}, f32[8,128]{1,0:T(8,128)S(1)}) custom-call(f32[8,256]{1,0:T(8,128)S(1)} %copy-done.1, s32[8,256]{1,0:T(8,128)S(1)} %copy-done.2, f32[1,256]{1,0:T(1,128)S(1)} %bitcast.3, f32[256,256]{1,0:T(8,128)S(1)} %copy-done, f32[1,256]{1,0:T(1,128)S(1)} %bitcast.4, f32[1,256]{1,0:T(1,128)S(1)} %bitcast.5), custom_call_target="tpu_custom_call" | custom-call | tf_op jit(solution)/shard_map/smoother/pallas_call | solution.py:448
  64.1 0.6 copy.10
  64.7 0.6 copy.11
Async XLA Ops:
  0.6 0.7 %copy-start.4 = (f32[256]{0:T(256)S(1)}, f32[256]{0:T(256)}, u32[]{:S(2)}) copy-start(f32[256]{0:T(256)} %param.10) | copy-start | bytes 3076
  0.6 0.7 %copy-start.5 = (f32[256]{0:T(256)S(1)}, f32[256]{0:T(256)}, u32[]{:S(2)}) copy-start(f32[256]{0:T(256)} %param.11) | copy-start | bytes 3076
  0.7 0.7 %copy-start.3 = (f32[256]{0:T(256)S(1)}, f32[256]{0:T(256)}, u32[]{:S(2)}) copy-start(f32[256]{0:T(256)} %param.8) | copy-start | bytes 3076
  1.3 0.9 %copy-start = (f32[256,256]{1,0:T(8,128)S(1)}, f32[256,256]{1,0:T(8,128)}, u32[]{:S(2)}) copy-start(f32[256,256]{1,0:T(8,128)} %trans_hbm.1) | copy-start | bytes 786436
  2.3 0.7 %copy-start.1 = (f32[8,256]{1,0:T(8,128)S(1)}, f32[8,256]{1,0:T(8,128)}, u32[]{:S(2)}) copy-start(f32[8,256]{1,0:T(8,128)} %obs_hbm.1) | copy-start | bytes 24580
  3.0 0.7 %copy-start.2 = (s32[8,256]{1,0:T(8,128)S(1)}, s32[8,256]{1,0:T(8,128)}, u32[]{:S(2)}) copy-start(s32[8,256]{1,0:T(8,128)} %mask_hbm.1) | copy-start | bytes 24580

commit v3 on v2

--- a/solution.py
+++ b/solution.py
@@ -12,6 +12,7 @@
 DAYS = 8
 XN, YN, ZN = 4, 4, 16
 QN = 4
+WORKER = (1, 4, 8, 12)
 CH = 4
 QD = CH * DAYS
 RINGS = XN * YN
@@ -43,7 +44,7 @@
 
 
 def kernel(
-    obs_hbm, mask_hbm, gain_hbm, trans_hbm, scale_hbm, init_hbm, filt_out, smooth_out,
+    obs_hbm, mask_hbm, gain_hbm, trans_hbm, scale_hbm, init_hbm, both_out,
     obs, mask, gain, trans, scale, init,
     rf, atf, athi, atlo, hp, hphi, hplo, xt, mk, khi, klo, mv, vo, vhi, vlo, sm, tm, pre, thi, tlo, pc, phi, plo,
     nb, nhi, nlo, ret4, frc4, gin, gout, ent, st, fs, fb, sb, wb, vb, eb,
@@ -56,7 +57,16 @@
     x, z = lax.div(seg, ZN), lax.rem(seg, ZN)
     q, r = lax.div(z, CH), lax.rem(z, CH)
     other = 1 - c
-    is_worker = r == 0
+
+    def place(k):
+        return jnp.where(
+            k < 2,
+            jnp.where(k == 0, WORKER[0], WORKER[1]),
+            jnp.where(k == 2, WORKER[2], WORKER[3]),
+        )
+
+    wz = place(q)
+    is_worker = z == wz
 
     fetches = [
         pltpu.make_async_copy(src, dst, in_sem.at[k])
@@ -92,7 +102,7 @@
         )
 
     def ring_peer(d):
-        return at(x, y, lax.rem(q + d, QN) * CH, c)
+        return at(x, y, place(lax.rem(q + d, QN)), c)
 
     def plane_peer(k):
         return at(lax.rem(x + k % XN, XN), lax.rem(y + k // XN, YN), z, c)
@@ -100,7 +110,7 @@
     @pl.when(is_worker)
     def _():
         for k in range(1, CH):
-            greet(at(x, y, z + k, c))
+            greet(at(x, y, q * CH + lax.rem(r + k, CH), c))
         for k in range(1, QN):
             greet(ring_peer(k))
         for k in range(1, RINGS):
@@ -109,7 +119,7 @@
 
     @pl.when(jnp.logical_not(is_worker))
     def _():
-        greet(at(x, y, q * CH, c))
+        greet(at(x, y, wz, c))
 
     for fetch in fetches[:3]:
         fetch.wait()
@@ -120,15 +130,15 @@
     @pl.when(jnp.logical_not(is_worker))
     def _():
         pl.semaphore_wait(barrier, 1)
-        to_worker = copy(rf.at[r], rf.at[r], m_send, m_recv.at[r], at(x, y, q * CH, c))
+        to_worker = copy(rf.at[r], rf.at[r], m_send, m_recv.at[r], at(x, y, wz, c))
         to_worker.start()
         for fetch in fetches[3:]:
             fetch.wait()
         to_worker.wait_send()
         arrival(frecv, m_send, of_recv).wait_recv()
-        filt_out[...] = frecv[...]
+        both_out[0:DAYS] = frecv[...]
         arrival(srecv, m_send, os_recv).wait_recv()
-        smooth_out[...] = srecv[...]
+        both_out[DAYS:] = srecv[...]
 
     @pl.when(is_worker)
     def _():
@@ -153,6 +163,12 @@
 
             return lax.fori_loop(first, DAYS, day, rows)
 
+        def chunk_here(k):
+            @pl.when(r != k)
+            def _():
+                arrival(rf.at[k], m_send, m_recv.at[k]).wait_recv()
+
+        chunk_here(0)
         rows = jnp.concatenate(
             [
                 atf[pl.ds(pl.multiple_of(c * HALF, HALF), HALF), :] * rf[0, 0:1, :],
@@ -163,7 +179,7 @@
         xt[0] = rows
         rows = advance(0, 1, rows)
         for k in range(1, CH):
-            arrival(rf.at[k], m_send, m_recv.at[k]).wait_recv()
+            chunk_here(k)
             rows = advance(k, 0, rows)
         mk[q, c] = rows
 
@@ -328,8 +344,10 @@
         v = (mm(st[0], vhi[0], vlo[0]) + vo[0, 0:1, :])[0:1, :]
         boundary = mm(gout[...], athi[...], atlo[...])
         me = y * XN + x
-        sub8 = lax.broadcasted_iota(jnp.int32, (8, M), 0)
-        vb[me] = jnp.where(sub8 == 0, v, boundary)
+        vb[me] = jnp.concatenate(
+            [v[:, :HALF], v[:, HALF:], boundary[0:1, :HALF], boundary[0:5, HALF:]],
+            0,
+        )
 
         def to_plane(k):
             return copy(vb.at[me], vb.at[me], v_send.at[k], v_recv.at[me], plane_peer(k))
@@ -363,13 +381,17 @@
             fh[...] = fb[:, HALF:M]
 
         def out_copy(src, dst, send, recv, k):
+            chip = lax.rem(r + k, CH)
             return copy(
-                src.at[pl.ds(k * DAYS, DAYS)], dst, send.at[k], recv, at(x, y, z + k, c)
+                src.at[pl.ds(pl.multiple_of(chip * DAYS, DAYS), DAYS)], dst, send.at[k], recv,
+                at(x, y, q * CH + chip, c),
             )
+
+        own_days = pl.ds(pl.multiple_of(r * DAYS, DAYS), DAYS)
 
         for k in (3, 2, 1):
             out_copy(fh, frecv, of_send, of_recv, k).start()
-        filt_out[...] = fh[0:DAYS, :]
+        both_out[0:DAYS] = fh[own_days, :]
 
         sb[0:QD, :] = fb[...] * weight
         sb[QD : 2 * QD, :] = jnp.zeros((QD, M), F32)
@@ -380,9 +402,11 @@
         for k in plane:
             src = lax.rem(y + k // XN, YN) * XN + lax.rem(x + k % XN, XN)
             arrival(vb.at[src], v_send.at[k], v_recv.at[src]).wait_recv()
-        for k in range(1, RINGS):
-            eb[k - 1 : k, :] = vb[k, 0:1, :]
-        eb[RINGS - 1 : RINGS, :] = vb[RINGS - 1, 1:2, :]
+        for half in range(2):
+            part = slice(half * HALF, (half + 1) * HALF)
+            for k in range(1, RINGS):
+                eb[k - 1 : k, part] = vb[k, half : half + 1, :]
+            eb[RINGS - 1 : RINGS, part] = vb[RINGS - 1, 2 + half : 3 + half, :]
         for k in range(4):
             eb[0:16, :] = eb[0:16, :] + mm(eb[1 << k : (1 << k) + 16, :], hphi[7 + k], hplo[7 + k])
         behind = jnp.broadcast_to(eb[pl.ds(me, 1), :], (8, M))
@@ -409,7 +433,7 @@
 
         for k in (3, 2, 1):
             out_copy(sh, srecv, os_send, os_recv, k).start()
-        smooth_out[...] = sh[0:DAYS, :]
+        both_out[DAYS:] = sh[own_days, :]
 
         for d in range(1, QN):
             ring_send(mk, k_send, k_recv, d).wait_send()
@@ -444,12 +468,12 @@
     def halves(*shape):
         return [buf(*shape, dtype=BF16), buf(*shape, dtype=BF16)]
 
-    out = jax.ShapeDtypeStruct((DAYS, HALF), F32)
-    return pl.pallas_call(
+    out = jax.ShapeDtypeStruct((2 * DAYS, HALF), F32)
+    both = pl.pallas_call(
         kernel,
-        out_shape=(out, out),
+        out_shape=out,
         in_specs=[hbm] * 6,
-        out_specs=(vmem, vmem),
+        out_specs=vmem,
         scratch_shapes=[
             buf(DAYS, M), buf(DAYS, M, dtype=jnp.int32), buf(1, M), buf(M, M), buf(1, M), buf(1, M),
             buf(CH, 2 * DAYS, M), buf(M, M), *halves(M, M),
@@ -463,7 +487,7 @@
             buf(DAYS, 8, M), buf(DAYS, 8, M),
             buf(8, M), buf(8, M), buf(XN, 8, M), buf(QN, 8, M),
             buf(8, M), buf(QD, M), buf(2 * QD, M), buf(QD, M),
-            buf(RINGS, 8, M), buf(32, M),
+            buf(RINGS, 8, HALF), buf(32, M),
             buf(QD, HALF), buf(QD, HALF), buf(DAYS, HALF), buf(DAYS, HALF),
             dma((6,)), dma, dma((CH,)),
             dma((QN,)), dma((QN,)), dma((QN,)), dma((QN,)),
@@ -481,6 +505,7 @@
         observations, masks, gains.reshape(1, M), transition,
         smoother_scale.reshape(1, M), initial_mean.reshape(1, M),
     )
+    return both[:DAYS], both[DAYS:]
 
 
 def solution(mesh):

time: 65.6 us -> 62.4 us (0.951)
  the two profiles are of different devices: /device:TPU:32 before, /device:TPU:8 now
where the time goes in v3:
time: 62.4 us; the launch traced here: 62.2 us
  Pallas kernels  57.9 us (93%)
  local copies, waits for them, and re-layouts  3.63 us (6%)
  between operations  0.67 us (1%)
    pallas_call x1, Pallas kernels, shards(): pl.pallas_call(kernel, out_shape=out, in_specs=[hbm] * 6, out_specs=vmem,...  57.9 us
    unnamed x12, local copies, waits for them, and re-layouts  3.03 us

profile of v3, /device:TPU:8, one launch (start us, length us, event | category | flops | bytes accessed | tf_op | source)
XLA Modules:
  0.0 62.2 jit_solution(5628484713082213510)
XLA Ops:
  0.6 0.0 copy-start.4
  0.6 0.0 copy-start.5
  0.7 0.0 copy-start.3
  0.7 0.7 %copy-done.4 = f32[256]{0:T(256)S(1)} copy-done((f32[256]{0:T(256)S(1)}, f32[256]{0:T(256)}, u32[]{:S(2)}) %copy-start.4) | copy-done | bytes 1048
  1.3 0.0 copy-done.5
  1.3 0.0 copy-done.3
  1.3 0.0 copy-start
  1.3 0.9 %copy-done = f32[256,256]{1,0:T(8,128)S(1)} copy-done((f32[256,256]{1,0:T(8,128)S(1)}, f32[256,256]{1,0:T(8,128)}, u32[]{:S(2)}) %copy-start) | copy-done | bytes 262168
  2.3 0.0 copy-start.1
  2.3 0.7 %copy-done.1 = f32[8,256]{1,0:T(8,128)S(1)} copy-done((f32[8,256]{1,0:T(8,128)S(1)}, f32[8,256]{1,0:T(8,128)}, u32[]{:S(2)}) %copy-start.1) | copy-done | bytes 8216
  3.0 0.0 copy-start.2
  3.0 0.7 %copy-done.2 = s32[8,256]{1,0:T(8,128)S(1)} copy-done((s32[8,256]{1,0:T(8,128)S(1)}, s32[8,256]{1,0:T(8,128)}, u32[]{:S(2)}) %copy-start.2) | copy-done | bytes 8216
  3.7 57.9 %smoother.1 = f32[16,128]{1,0:T(8,128)S(1)} custom-call(f32[8,256]{1,0:T(8,128)S(1)} %copy-done.1, s32[8,256]{1,0:T(8,128)S(1)} %copy-done.2, f32[1,256]{1,0:T(1,128)S(1)} %bitcast.3, f32[256,256]{1,0:T(8,128)S(1)} %copy-done, f32[1,256]{1,0:T(1,128)S(1)} %bitcast.4, f32[1,256]{1,0:T(1,128)S(1)} %bitcast.5), custom_call_target="tpu_custom_call" | custom-call | tf_op jit(solution)/shard_map/smoother/pallas_call | solution.py:472
  61.6 0.6 fusion
Async XLA Ops:
  0.6 0.7 %copy-start.4 = (f32[256]{0:T(256)S(1)}, f32[256]{0:T(256)}, u32[]{:S(2)}) copy-start(f32[256]{0:T(256)} %param.10) | copy-start | bytes 3076
  0.6 0.7 %copy-start.5 = (f32[256]{0:T(256)S(1)}, f32[256]{0:T(256)}, u32[]{:S(2)}) copy-start(f32[256]{0:T(256)} %param.11) | copy-start | bytes 3076
  0.7 0.7 %copy-start.3 = (f32[256]{0:T(256)S(1)}, f32[256]{0:T(256)}, u32[]{:S(2)}) copy-start(f32[256]{0:T(256)} %param.8) | copy-start | bytes 3076
  1.3 0.9 %copy-start = (f32[256,256]{1,0:T(8,128)S(1)}, f32[256,256]{1,0:T(8,128)}, u32[]{:S(2)}) copy-start(f32[256,256]{1,0:T(8,128)} %trans_hbm.1) | copy-start | bytes 786436
  2.3 0.7 %copy-start.1 = (f32[8,256]{1,0:T(8,128)S(1)}, f32[8,256]{1,0:T(8,128)}, u32[]{:S(2)}) copy-start(f32[8,256]{1,0:T(8,128)} %obs_hbm.1) | copy-start | bytes 24580
  3.0 0.7 %copy-start.2 = (s32[8,256]{1,0:T(8,128)S(1)}, s32[8,256]{1,0:T(8,128)}, u32[]{:S(2)}) copy-start(s32[8,256]{1,0:T(8,128)} %mask_hbm.1) | copy-start | bytes 24580

commit v4 on v3

--- a/solution.py
+++ b/solution.py
@@ -47,7 +47,7 @@
     obs_hbm, mask_hbm, gain_hbm, trans_hbm, scale_hbm, init_hbm, both_out,
     obs, mask, gain, trans, scale, init,
     rf, atf, athi, atlo, hp, hphi, hplo, xt, mk, khi, klo, mv, vo, vhi, vlo, sm, tm, pre, thi, tlo, pc, phi, plo,
-    nb, nhi, nlo, ret4, frc4, gin, gout, ent, st, fs, fb, sb, wb, vb, eb,
+    exhi, exlo, eyhi, eylo, nb, nhi, nlo, ret4, frc4, gin, gout, ent, st, fs, fb, sb, wb, vb, eb,
     fh, sh, frecv, srecv,
     in_sem, m_send, m_recv, k_send, k_recv, ks_send, ks_recv, w_send, w_recv, ws_send, ws_recv,
     p_send, p_recv, n_send, n_recv, ns_send, ns_recv, g_send, g_recv, v_send, v_recv,
@@ -148,9 +148,6 @@
         at_full = trans[...].T
         atf[...] = at_full
         athi[...], atlo[...] = split(at_full)
-        h0 = trans[...] * scale[...]
-        hp[...] = h0
-        hphi[0], hplo[0] = split(h0)
 
         def advance(chip, first, rows):
             def day(j, rows):
@@ -161,7 +158,9 @@
                 xt[chip * DAYS + j] = rows
                 return rows
 
-            return lax.fori_loop(first, DAYS, day, rows)
+            for j in range(first, DAYS):
+                rows = day(j, rows)
+            return rows
 
         def chunk_here(k):
             @pl.when(r != k)
@@ -197,6 +196,10 @@
 
         def chunk_share(k):
             return copy(xt.at[k * DAYS - 1], pc.at[k - 1], p_send.at[k - 1], p_recv.at[k - 1], sibling)
+
+        h0 = trans[...] * scale[...]
+        hp[...] = h0
+        hphi[0], hplo[0] = split(h0)
 
         for k in range(1, CH):
             chunk_share(k).start()
@@ -246,6 +249,14 @@
             return 0
 
         lax.fori_loop(1, POWERS, square, 0)
+
+        def power(k):
+            return hphi[k].astype(F32) + hplo[k].astype(F32)
+
+        exhi[0], exlo[0] = hphi[0], hplo[0]
+        exhi[1], exlo[1] = split(mm(power(3), hphi[0], hplo[0]))
+        exhi[2], exlo[2] = split(mm(power(4), hphi[0], hplo[0]))
+        exhi[3], exlo[3] = split(mm(power(4), exhi[1], exlo[1]))
         ret4[...] = jnp.zeros_like(ret4)
         frc4[...] = jnp.zeros_like(frc4)
         for k in range(CH):
@@ -306,6 +317,42 @@
         def to_group():
             return copy(gout, gin, g_send, g_recv, at(x, lax.rem(y + 1, YN), z, c))
 
+        left = QN - 1 - q
+
+        def behind_quads():
+            def fold(k, _):
+                for bit in range(2):
+                    src = (exhi, exlo) if bit == 0 else (eyhi, eylo)
+
+                    @pl.when(lax.rem(lax.div(left, 1 << bit), 2) == 1)
+                    def _():
+                        whole_map = src[0][k].astype(F32) + src[1][k].astype(F32)
+                        eyhi[k], eylo[k] = split(mm(whole_map, hphi[5 + bit], hplo[5 + bit]))
+
+                    if bit == 0:
+
+                        @pl.when(lax.rem(left, 2) == 0)
+                        def _():
+                            eyhi[k], eylo[k] = exhi[k], exlo[k]
+
+                return 0
+
+            lax.fori_loop(0, CH, fold, 0)
+
+        def expand(vector, xhi, xlo):
+            first = jnp.concatenate(
+                [mm(vector, xhi[k], xlo[k])[0:1, :] for k in range(CH)]
+                + [jnp.zeros((8 - CH, M), F32)],
+                0,
+            )
+            found = first
+            for k in range(3):
+                found = jnp.concatenate([found, mm(found, hphi[k], hplo[k])], 0)
+            for k in range(CH):
+                for j in range(DAYS):
+                    t = QD - 1 - DAYS * k - j
+                    wb[t : t + 1, :] = found[8 * j + k : 8 * j + k + 1, :]
+
         @pl.when(y == 0)
         def _():
             state = jnp.broadcast_to(init[...], (8, M))
@@ -323,6 +370,10 @@
         @pl.when(y > 1)
         def _():
             smoother_map()
+
+        @pl.when(y == YN - 1)
+        def _():
+            behind_quads()
 
         @pl.when(y > 0)
         def _():
@@ -398,6 +449,13 @@
         for k in range(5):
             sb[0:QD, :] = sb[0:QD, :] + mm(sb[1 << k : (1 << k) + QD, :], hphi[k], hplo[k])
 
+        @pl.when(y < YN - 1)
+        def _():
+            behind_quads()
+
+        expand(jnp.where(left > 0, after, 0.0), exhi, exlo)
+        sb[0:QD, :] = sb[0:QD, :] + wb[...]
+
         eb[...] = jnp.zeros_like(eb)
         for k in plane:
             src = lax.rem(y + k // XN, YN) * XN + lax.rem(x + k % XN, XN)
@@ -410,17 +468,7 @@
         for k in range(4):
             eb[0:16, :] = eb[0:16, :] + mm(eb[1 << k : (1 << k) + 16, :], hphi[7 + k], hplo[7 + k])
         behind = jnp.broadcast_to(eb[pl.ds(me, 1), :], (8, M))
-        left = QN - 1 - q
-        behind = jnp.where(lax.rem(left, 2) == 1, mm(behind, hphi[5], hplo[5]), behind)
-        behind = jnp.where(left >= 2, mm(behind, hphi[6], hplo[6]), behind)
-        behind = jnp.where(left > 0, behind + after, behind)
-
-        wb[QD - 8 : QD, :] = jnp.zeros((8, M), F32)
-        wb[QD - 1 : QD, :] = mm(behind, hphi[0], hplo[0])[0:1, :]
-        for k in range(5):
-            n = 1 << k
-            m = max(n, 8)
-            wb[QD - 2 * n : QD - n, :] = mm(wb[QD - m : QD, :], hphi[k], hplo[k])[m - n : m, :]
+        expand(behind, eyhi, eylo)
         total = sb[0:QD, :] + wb[...]
 
         @pl.when(c == 0)
@@ -483,6 +531,7 @@
             buf(QN, 2, ROWS, M), buf(2, 8, M), *halves(2, M, M),
             buf(M + 8, M), buf(M + 8, M), buf(M + 8, M), *halves(2, M, M),
             buf(CH - 1, ROWS, M), *halves(CH - 1, M, M),
+            *halves(CH, M, M), *halves(CH, M, M),
             buf(XN, 2, ROWS, M), *halves(XN, M, M),
             buf(DAYS, 8, M), buf(DAYS, 8, M),
             buf(8, M), buf(8, M), buf(XN, 8, M), buf(QN, 8, M),

time: 62.4 us -> 61 us (0.978)
  Pallas kernels: 57.9 us -> 56.4 us
    pallas_call x1, Pallas kernels: 57.9 us -> 56.4 us  [shards(): pl.pallas_call(kernel, out_shape=out, in_specs=[hbm] * 6, out_specs=vmem,...]
where the time goes in v4:
time: 61 us; the launch traced here: 60.7 us
  Pallas kernels  56.4 us (92%)
  local copies, waits for them, and re-layouts  3.63 us (6%)
  between operations  0.67 us (1%)
    pallas_call x1, Pallas kernels, shards(): pl.pallas_call(kernel, out_shape=out, in_specs=[hbm] * 6, out_specs=vmem,...  56.4 us
    unnamed x12, local copies, waits for them, and re-layouts  3.03 us

profile of v4, /device:TPU:8, one launch (start us, length us, event | category | flops | bytes accessed | tf_op | source)
XLA Modules:
  0.0 60.7 jit_solution(4024938152476417076)
XLA Ops:
  0.6 0.0 copy-start.4
  0.6 0.0 copy-start.5
  0.7 0.0 copy-start.3
  0.7 0.7 %copy-done.4 = f32[256]{0:T(256)S(1)} copy-done((f32[256]{0:T(256)S(1)}, f32[256]{0:T(256)}, u32[]{:S(2)}) %copy-start.4) | copy-done | bytes 1048
  1.3 0.0 copy-done.5
  1.3 0.0 copy-done.3
  1.3 0.0 copy-start
  1.3 0.9 %copy-done = f32[256,256]{1,0:T(8,128)S(1)} copy-done((f32[256,256]{1,0:T(8,128)S(1)}, f32[256,256]{1,0:T(8,128)}, u32[]{:S(2)}) %copy-start) | copy-done | bytes 262168
  2.3 0.0 copy-start.1
  2.3 0.7 %copy-done.1 = f32[8,256]{1,0:T(8,128)S(1)} copy-done((f32[8,256]{1,0:T(8,128)S(1)}, f32[8,256]{1,0:T(8,128)}, u32[]{:S(2)}) %copy-start.1) | copy-done | bytes 8216
  3.0 0.0 copy-start.2
  3.0 0.7 %copy-done.2 = s32[8,256]{1,0:T(8,128)S(1)} copy-done((s32[8,256]{1,0:T(8,128)S(1)}, s32[8,256]{1,0:T(8,128)}, u32[]{:S(2)}) %copy-start.2) | copy-done | bytes 8216
  3.7 56.4 %smoother.1 = f32[16,128]{1,0:T(8,128)S(1)} custom-call(f32[8,256]{1,0:T(8,128)S(1)} %copy-done.1, s32[8,256]{1,0:T(8,128)S(1)} %copy-done.2, f32[1,256]{1,0:T(1,128)S(1)} %bitcast.3, f32[256,256]{1,0:T(8,128)S(1)} %copy-done, f32[1,256]{1,0:T(1,128)S(1)} %bitcast.4, f32[1,256]{1,0:T(1,128)S(1)} %bitcast.5), custom_call_target="tpu_custom_call" | custom-call | tf_op jit(solution)/shard_map/smoother/pallas_call | solution.py:520
  60.1 0.6 fusion
Async XLA Ops:
  0.6 0.7 %copy-start.4 = (f32[256]{0:T(256)S(1)}, f32[256]{0:T(256)}, u32[]{:S(2)}) copy-start(f32[256]{0:T(256)} %param.10) | copy-start | bytes 3076
  0.6 0.7 %copy-start.5 = (f32[256]{0:T(256)S(1)}, f32[256]{0:T(256)}, u32[]{:S(2)}) copy-start(f32[256]{0:T(256)} %param.11) | copy-start | bytes 3076
  0.7 0.7 %copy-start.3 = (f32[256]{0:T(256)S(1)}, f32[256]{0:T(256)}, u32[]{:S(2)}) copy-start(f32[256]{0:T(256)} %param.8) | copy-start | bytes 3076
  1.3 0.9 %copy-start = (f32[256,256]{1,0:T(8,128)S(1)}, f32[256,256]{1,0:T(8,128)}, u32[]{:S(2)}) copy-start(f32[256,256]{1,0:T(8,128)} %trans_hbm.1) | copy-start | bytes 786436
  2.3 0.7 %copy-start.1 = (f32[8,256]{1,0:T(8,128)S(1)}, f32[8,256]{1,0:T(8,128)}, u32[]{:S(2)}) copy-start(f32[8,256]{1,0:T(8,128)} %obs_hbm.1) | copy-start | bytes 24580
  3.0 0.7 %copy-start.2 = (s32[8,256]{1,0:T(8,128)S(1)}, s32[8,256]{1,0:T(8,128)}, u32[]{:S(2)}) copy-start(s32[8,256]{1,0:T(8,128)} %mask_hbm.1) | copy-start | bytes 24580

commit v5 on v4

--- a/solution.py
+++ b/solution.py
@@ -27,6 +27,9 @@
 
 def mm(v, whi, wlo):
     rows = v.shape[0]
+    if rows == ROWS:
+        cuts = (0, HALF // 2, HALF, ROWS)
+        return jnp.concatenate([mm(v[i:j], whi, wlo) for i, j in zip(cuts, cuts[1:])], 0)
     if rows % 16 == 8 and rows > 8:
         return jnp.concatenate([mm(v[: rows - 8], whi, wlo), mm(v[rows - 8 :], whi, wlo)], 0)
     hi, lo = split(v)

time: 61 us -> 60.7 us (level)
  no operation moved by 1% of the time
where the time goes in v5:
time: 60.7 us; the launch traced here: 60.5 us
  Pallas kernels  56.2 us (93%)
  local copies, waits for them, and re-layouts  3.63 us (6%)
  between operations  0.67 us (1%)
    pallas_call x1, Pallas kernels, shards(): pl.pallas_call(kernel, out_shape=out, in_specs=[hbm] * 6, out_specs=vmem,...  56.2 us
    unnamed x12, local copies, waits for them, and re-layouts  3.03 us

profile of v5, /device:TPU:8, one launch (start us, length us, event | category | flops | bytes accessed | tf_op | source)
XLA Modules:
  0.0 60.5 jit_solution(2341197327141234105)
XLA Ops:
  0.6 0.0 copy-start.4
  0.6 0.0 copy-start.5
  0.7 0.0 copy-start.3
  0.7 0.7 %copy-done.4 = f32[256]{0:T(256)S(1)} copy-done((f32[256]{0:T(256)S(1)}, f32[256]{0:T(256)}, u32[]{:S(2)}) %copy-start.4) | copy-done | bytes 1048
  1.3 0.0 copy-done.5
  1.3 0.0 copy-done.3
  1.3 0.0 copy-start
  1.3 0.9 %copy-done = f32[256,256]{1,0:T(8,128)S(1)} copy-done((f32[256,256]{1,0:T(8,128)S(1)}, f32[256,256]{1,0:T(8,128)}, u32[]{:S(2)}) %copy-start) | copy-done | bytes 262168
  2.3 0.0 copy-start.1
  2.3 0.7 %copy-done.1 = f32[8,256]{1,0:T(8,128)S(1)} copy-done((f32[8,256]{1,0:T(8,128)S(1)}, f32[8,256]{1,0:T(8,128)}, u32[]{:S(2)}) %copy-start.1) | copy-done | bytes 8216
  3.0 0.0 copy-start.2
  3.0 0.7 %copy-done.2 = s32[8,256]{1,0:T(8,128)S(1)} copy-done((s32[8,256]{1,0:T(8,128)S(1)}, s32[8,256]{1,0:T(8,128)}, u32[]{:S(2)}) %copy-start.2) | copy-done | bytes 8216
  3.7 56.2 %smoother.1 = f32[16,128]{1,0:T(8,128)S(1)} custom-call(f32[8,256]{1,0:T(8,128)S(1)} %copy-done.1, s32[8,256]{1,0:T(8,128)S(1)} %copy-done.2, f32[1,256]{1,0:T(1,128)S(1)} %bitcast.3, f32[256,256]{1,0:T(8,128)S(1)} %copy-done, f32[1,256]{1,0:T(1,128)S(1)} %bitcast.4, f32[1,256]{1,0:T(1,128)S(1)} %bitcast.5), custom_call_target="tpu_custom_call" | custom-call | tf_op jit(solution)/shard_map/smoother/pallas_call | solution.py:523
  59.9 0.6 fusion
Async XLA Ops:
  0.6 0.7 %copy-start.4 = (f32[256]{0:T(256)S(1)}, f32[256]{0:T(256)}, u32[]{:S(2)}) copy-start(f32[256]{0:T(256)} %param.10) | copy-start | bytes 3076
  0.6 0.7 %copy-start.5 = (f32[256]{0:T(256)S(1)}, f32[256]{0:T(256)}, u32[]{:S(2)}) copy-start(f32[256]{0:T(256)} %param.11) | copy-start | bytes 3076
  0.7 0.7 %copy-start.3 = (f32[256]{0:T(256)S(1)}, f32[256]{0:T(256)}, u32[]{:S(2)}) copy-start(f32[256]{0:T(256)} %param.8) | copy-start | bytes 3076
  1.3 0.9 %copy-start = (f32[256,256]{1,0:T(8,128)S(1)}, f32[256,256]{1,0:T(8,128)}, u32[]{:S(2)}) copy-start(f32[256,256]{1,0:T(8,128)} %trans_hbm.1) | copy-start | bytes 786436
  2.3 0.7 %copy-start.1 = (f32[8,256]{1,0:T(8,128)S(1)}, f32[8,256]{1,0:T(8,128)}, u32[]{:S(2)}) copy-start(f32[8,256]{1,0:T(8,128)} %obs_hbm.1) | copy-start | bytes 24580
  3.0 0.7 %copy-start.2 = (s32[8,256]{1,0:T(8,128)S(1)}, s32[8,256]{1,0:T(8,128)}, u32[]{:S(2)}) copy-start(s32[8,256]{1,0:T(8,128)} %mask_hbm.1) | copy-start | bytes 24580

commit v6 on v5

--- a/solution.py
+++ b/solution.py
@@ -204,15 +204,14 @@
         hp[...] = h0
         hphi[0], hplo[0] = split(h0)
 
+        weight = 1.0 - scale[...] * jnp.sum(trans[...] * trans[...], axis=0, keepdims=True)
+
+        def back(k, rows):
+            return xt[QD - 2 - k] * weight + mm(rows, hphi[0], hplo[0])
+
+        mv[q, c] = lax.fori_loop(0, QD - 1, back, xt[QD - 1] * weight)
         for k in range(1, CH):
             chunk_share(k).start()
-
-        weight = 1.0 - scale[...] * jnp.sum(trans[...] * trans[...], axis=0, keepdims=True)
-
-        def back(k, rows):
-            return xt[QD - 2 - k] * weight + mm(rows, hphi[0], hplo[0])
-
-        mv[q, c] = lax.fori_loop(0, QD - 1, back, xt[QD - 1] * weight)
 
         for d in (1, 3, 2):
             k = lax.rem(q + d, QN)

time: 60.7 us -> 60.7 us (level)
  no operation moved by 1% of the time
where the time goes in v6:
time: 60.7 us; the launch traced here: 60.5 us
  Pallas kernels  56.2 us (93%)
  local copies, waits for them, and re-layouts  3.63 us (6%)
  between operations  0.67 us (1%)
    pallas_call x1, Pallas kernels, shards(): pl.pallas_call(kernel, out_shape=out, in_specs=[hbm] * 6, out_specs=vmem,...  56.2 us
    unnamed x12, local copies, waits for them, and re-layouts  3.03 us

profile of v6, /device:TPU:8, one launch (start us, length us, event | category | flops | bytes accessed | tf_op | source)
XLA Modules:
  0.0 60.5 jit_solution(3078516001128762921)
XLA Ops:
  0.6 0.0 copy-start.4
  0.6 0.0 copy-start.5
  0.7 0.0 copy-start.3
  0.7 0.7 %copy-done.4 = f32[256]{0:T(256)S(1)} copy-done((f32[256]{0:T(256)S(1)}, f32[256]{0:T(256)}, u32[]{:S(2)}) %copy-start.4) | copy-done | bytes 1048
  1.3 0.0 copy-done.5
  1.3 0.0 copy-done.3
  1.3 0.0 copy-start
  1.3 0.9 %copy-done = f32[256,256]{1,0:T(8,128)S(1)} copy-done((f32[256,256]{1,0:T(8,128)S(1)}, f32[256,256]{1,0:T(8,128)}, u32[]{:S(2)}) %copy-start) | copy-done | bytes 262168
  2.3 0.0 copy-start.1
  2.3 0.7 %copy-done.1 = f32[8,256]{1,0:T(8,128)S(1)} copy-done((f32[8,256]{1,0:T(8,128)S(1)}, f32[8,256]{1,0:T(8,128)}, u32[]{:S(2)}) %copy-start.1) | copy-done | bytes 8216
  3.0 0.0 copy-start.2
  3.0 0.7 %copy-done.2 = s32[8,256]{1,0:T(8,128)S(1)} copy-done((s32[8,256]{1,0:T(8,128)S(1)}, s32[8,256]{1,0:T(8,128)}, u32[]{:S(2)}) %copy-start.2) | copy-done | bytes 8216
  3.7 56.2 %smoother.1 = f32[16,128]{1,0:T(8,128)S(1)} custom-call(f32[8,256]{1,0:T(8,128)S(1)} %copy-done.1, s32[8,256]{1,0:T(8,128)S(1)} %copy-done.2, f32[1,256]{1,0:T(1,128)S(1)} %bitcast.3, f32[256,256]{1,0:T(8,128)S(1)} %copy-done, f32[1,256]{1,0:T(1,128)S(1)} %bitcast.4, f32[1,256]{1,0:T(1,128)S(1)} %bitcast.5), custom_call_target="tpu_custom_call" | custom-call | tf_op jit(solution)/shard_map/smoother/pallas_call | solution.py:522
  59.9 0.6 fusion
Async XLA Ops:
  0.6 0.7 %copy-start.4 = (f32[256]{0:T(256)S(1)}, f32[256]{0:T(256)}, u32[]{:S(2)}) copy-start(f32[256]{0:T(256)} %param.10) | copy-start | bytes 3076
  0.6 0.7 %copy-start.5 = (f32[256]{0:T(256)S(1)}, f32[256]{0:T(256)}, u32[]{:S(2)}) copy-start(f32[256]{0:T(256)} %param.11) | copy-start | bytes 3076
  0.7 0.7 %copy-start.3 = (f32[256]{0:T(256)S(1)}, f32[256]{0:T(256)}, u32[]{:S(2)}) copy-start(f32[256]{0:T(256)} %param.8) | copy-start | bytes 3076
  1.3 0.9 %copy-start = (f32[256,256]{1,0:T(8,128)S(1)}, f32[256,256]{1,0:T(8,128)}, u32[]{:S(2)}) copy-start(f32[256,256]{1,0:T(8,128)} %trans_hbm.1) | copy-start | bytes 786436
  2.3 0.7 %copy-start.1 = (f32[8,256]{1,0:T(8,128)S(1)}, f32[8,256]{1,0:T(8,128)}, u32[]{:S(2)}) copy-start(f32[8,256]{1,0:T(8,128)} %obs_hbm.1) | copy-start | bytes 24580
  3.0 0.7 %copy-start.2 = (s32[8,256]{1,0:T(8,128)S(1)}, s32[8,256]{1,0:T(8,128)}, u32[]{:S(2)}) copy-start(s32[8,256]{1,0:T(8,128)} %mask_hbm.1) | copy-start | bytes 24580
